TPU v7x, 32 devices: a whole 2x2x4 slice. The times are simulated.
32 devices in a mesh: grp: 2 (over x), inner: 16 (over z, y, core).
Axes of the slice: x: 2, y: 2, z: 4, core: 2. Of those that a mesh axis runs over, the one named last changes fastest.
Arguments:
- tokens: bfloat16 [128, 8192], P(('grp', 'inner')), parts along dimension 0, may hold values from -6 to 6
- token_scale: bfloat16 [128], P(('grp', 'inner')), parts along dimension 0, may hold values from 0.5 to 2
- gate_weight: bfloat16 [8192, 26624], P(None, 'inner'), may hold values from -0.0625 to 0.0625
- up_weight: bfloat16 [8192, 26624], P(None, 'inner'), may hold values from -0.0625 to 0.0625
- gate_scale: float32 [26624], P('inner'), may hold values from 0.5 to 2
- up_scale: float32 [26624], P('inner'), may hold values from 0.5 to 2
- down_weight: bfloat16 [26624, 8192], P('inner'), may hold values from -0.0390625 to 0.0390625
- down_scale: float32 [8192], replicated, may hold values from 0.5 to 2
Outputs:
- mixed: bfloat16 [128, 8192], P(('grp', 'inner')), parts along dimension 0
There are 2 independent parts, one for each index of `grp`. A program takes and returns all parts, laid end to end along the dimension named above; an argument that names none is the same for every part. Nothing has to cross between parts.
All inputs are finite; a program needn't handle non-finite values.
Results may differ from a plain program's by a relative error of at most 0.0049.
Values may be sent and summed in bfloat16 or wider, within the bound.
A program may use at most 192 MiB of HBM per device.

v0:
```python
import jax
import jax.numpy as jnp
from jax import lax
from jax.sharding import PartitionSpec as P


def local(
    tokens, token_scale, gate_weight, up_weight, gate_scale, up_scale, down_weight, down_scale
):
    pieces = lax.all_gather((tokens, token_scale), "inner", axis=0, tiled=True)
    token_codes = pieces[0]
    factor = pieces[1].astype(jnp.float32)[:, None]
    gate = (
        jnp.dot(token_codes, gate_weight, preferred_element_type=jnp.float32)
        * factor
        * gate_scale[None, :]
    )
    up = (
        jnp.dot(token_codes, up_weight, preferred_element_type=jnp.float32)
        * factor
        * up_scale[None, :]
    )
    hidden = (jax.nn.silu(gate) * up).astype(jnp.bfloat16)
    summed = lax.psum_scatter(
        jnp.dot(hidden, down_weight, preferred_element_type=jnp.float32),
        "inner",
        scatter_dimension=0,
        tiled=True,
    )
    return (summed * down_scale[None, :]).astype(jnp.bfloat16)


def solution(mesh):
    return jax.shard_map(
        local,
        mesh=mesh,
        in_specs=(
            P(("grp", "inner"), None),
            P(("grp", "inner")),
            P(None, "inner"),
            P(None, "inner"),
            P("inner"),
            P("inner"),
            P("inner", None),
            P(),
        ),
        out_specs=P(("grp", "inner"), None),
        check_vma=False,
    )
```

profile of v0, /device:TPU:0, one launch (start us, length us, event | category | flops | bytes accessed | tf_op | source)
XLA Modules:
  0.0 190.2 jit_solution(15827916442015741837)
XLA Ops:
  6.5 0.0 copy-start
  6.5 0.0 all-gather.3.cloned.1.call-start
  6.5 0.7 all-gather.3.cloned.1.call-update
  7.3 0.0 all-reduce.4.cloned.1.call-start
  7.3 1.3 fusion.15
  9.2 0.9 dynamic-update-slice
  10.1 35.1 %all-reduce = bf16[64]{0:T(256)(128)(2,1)S(1)} all-reduce(bf16[64]{0:T(256)(128)(2,1)S(1)} %dynamic-update-slice), channel_id=1, replica_groups=mesh['grp'=2,'inner'=16] {'inner'}, use_global_device_ids=true, to_apply=%add | all-reduce | flops 64 | bytes 256
  45.2 5.0 %all-gather.3.cloned.1.call-done = bf16[16,4,8192]{2,1,0:T(4,128)(2,1)} async-done(((bf16[1,4,8192]{2,1,0:T(4,128)(2,1)}), bf16[16,4,8192]{2,1,0:T(4,128)(2,1)}) %all-gather.3.cloned.1.call-update) | async-done | bytes 1048592 | tf_op jit(solution)/shard_map/all_gather | solution.py:10
  50.1 1.3 reshape.8
  51.5 11.3 %fusion.2 = f32[64,1664]{1,0:T(8,128)S(1)} fusion(bf16[64,8192]{1,0:T(8,128)(2,1)S(1)} %reshape.8, bf16[8192,1664]{1,0:T(8,128)(2,1)} %param.10, f32[1664]{0:T(1024)} %param.12, f32[64]{0:T(128)S(1)} %convert_element_type.9), kind=kOutput, calls=%fused_computation.4 | convolution fusion | flops 1745043456 | bytes 28744448 | tf_op jit(solution)/shard_map/dot_general | solution.py:14
  62.8 0.0 copy-done
  62.8 0.0 copy-start.1
  62.8 22.0 %fusion.4 = f32[64,8192]{1,0:T(8,128)} fusion(bf16[1664,8192]{1,0:T(8,128)(2,1)} %param.14, bf16[64,8192]{1,0:T(8,128)(2,1)S(1)} %reshape.8, bf16[8192,1664]{1,0:T(8,128)(2,1)} %param.11, f32[64,1664]{1,0:T(8,128)S(1)} %fusion.2, f32[1664]{0:T(1024)S(1)} %copy-done, f32[64]{0:T(128)S(1)} %convert_element_type.9), kind=kOutput, calls=%fused_computation.6 | convolution fusion | flops 3490512896 | bytes 58104576 | tf_op jit(solution)/shard_map/dot_general | solution.py:25
  84.8 0.0 all-reduce.4.cloned.1.call-update
  85.5 96.2 %all-reduce.4.cloned.1.call-done = f32[64,8192]{1,0:T(8,128)} async-done(((f32[64,8192]{1,0:T(8,128)}), f32[64,8192]{1,0:T(8,128)}) %all-reduce.4.cloned.1.call-update) | async-done | bytes 2097168
  181.7 0.0 copy-done.1
  181.7 1.6 fusion.13
  (2 shorter events, 0.0 us)
Async XLA Ops:
  6.5 56.3 %copy-start = (f32[1664]{0:T(1024)S(1)}, f32[1664]{0:T(1024)}, u32[]{:S(2)}) copy-start(f32[1664]{0:T(1024)} %param.13) | copy-start | bytes 19972
  6.5 43.6 %all-gather.3.cloned.1.call-start = ((), (), s32[]{:S(2)}) async-start(), calls=%async_computation | async-start | bytes 1114112 | tf_op jit(solution)/shard_map/all_gather | solution.py:10
  7.3 174.5 %all-reduce.4.cloned.1.call-start = ((), (), s32[]{:S(2)}) async-start(), calls=%async_computation.1 | async-start | bytes 4194304
  62.8 118.9 %copy-start.1 = (f32[8192]{0:T(1024)S(1)}, f32[8192]{0:T(1024)}, u32[]{:S(2)}) copy-start(f32[8192]{0:T(1024)} %param.15) | copy-start | bytes 98308
Sparse Core Ops, SparseCore 0:
  9.5 40.5 all-gather.2
  85.0 96.7 all-reduce.3
where the time goes:
time: 190 us
  waiting for transfers between devices  102 us (54%)
  blocking collectives  35.1 us (18%)
  matrix products  33.3 us (18%)
  between operations  14.7 us (8%)
  local copies, waits for them, and re-layouts  3.53 us (2%)
    unnamed x3, waiting for transfers between devices  97 us
    unnamed x1, blocking collectives  35.1 us
    dot_general x1, matrix products, local(): jnp.dot(hidden, down_weight, preferred_element_type=jnp.float32)  22 us
    dot_general x1, matrix products, local(): jnp.dot(token_codes, gate_weight, preferred_element_type=jnp.float32)  11.3 us
    all_gather x1, waiting for transfers between devices, local(): pieces = lax.all_gather((tokens, token_scale), 'inner', axis=0, tiled=True)  4.97 us
  transfers between devices with their start and end apart: 2, of which 2 were waited for; matrix products, arithmetic and copies ran while one was open for 1% of the time, Pallas kernels for 0%

commit v1 on v0

v1 whole, which is shorter than its diff:
```python
import jax
import jax.numpy as jnp
from jax import lax
from jax.experimental import pallas as pl
from jax.experimental.pallas import tpu as pltpu
from jax.sharding import PartitionSpec as P

MESH = pl.DeviceIdType.MESH
F32, BF16 = jnp.float32, jnp.bfloat16

FOLD = 4
TC = 4
NC = 8
NB = 5
Z, Y = 4, 2


def plain(
    tokens, token_scale, gate_weight, up_weight, gate_scale, up_scale, down_weight, down_scale
):
    pieces = lax.all_gather((tokens, token_scale), "inner", axis=0, tiled=True)
    token_codes = pieces[0]
    factor = pieces[1].astype(F32)[:, None]
    gate = (
        jnp.dot(token_codes, gate_weight, preferred_element_type=F32)
        * factor
        * gate_scale[None, :]
    )
    up = (
        jnp.dot(token_codes, up_weight, preferred_element_type=F32)
        * factor
        * up_scale[None, :]
    )
    hidden = (jax.nn.silu(gate) * up).astype(BF16)
    summed = lax.psum_scatter(
        jnp.dot(hidden, down_weight, preferred_element_type=F32),
        "inner",
        scatter_dimension=0,
        tiled=True,
    )
    return (summed * down_scale[None, :]).astype(BF16)


def kernel(
    tok, gw, uw, gs, us, dw, out,
    g0, g1, g2, g3, left, fac, gbuf, ubuf, dbuf, acc_g, acc_u, hid, full,
    part, s1s, s1r, part2, s2s, s2r, part3, s3s, s3r,
    wsem, dsem, zs, zr, h1s, h1r, h2s, h2r, cs, cr, hs, hr, r1s, r1r, r2s, r2r, r3s, r3r,
):
    x = lax.axis_index("grp")
    inner = lax.axis_index("inner")
    core, y, z = inner % 2, (inner // 2) % 2, inner // 4
    xf, yf = 1 - x, 1 - y

    def dev(xx, zz, yy, cc):
        return (xx, (zz * Y + yy) * 2 + cc)

    gathered = (g0, g1, g2, g3)
    width = fac.shape[1]
    kw = (tok.shape[1] - width) // TC
    half = hid.shape[3]
    ff = full.shape[2]
    rest = ff - half
    ncol = dbuf.shape[2]
    off = pl.multiple_of(x * rest, 128)

    def wcopy(c, which):
        src, dst = ((gw, gbuf), (uw, ubuf))[which]
        return pltpu.make_async_copy(
            src.at[:, pl.ds(c * kw, kw), pl.ds(off, half)], dst.at[c], wsem.at[which, c]
        )

    def dcopy(n):
        return pltpu.make_async_copy(
            dw.at[:, pl.ds(n * ncol, ncol)], dbuf.at[n % NB], dsem.at[n]
        )

    for c in range(TC):
        wcopy(c, 0).start()
        wcopy(c, 1).start()
    for n in range(NB):
        dcopy(n).start()

    col = x * 2 + y
    rows = pl.ds(pl.multiple_of(z * 16, 16), 16)
    g0[core, col, rows, pl.ds(0, kw)] = tok[:, pl.ds(0, kw)]
    g0[core, col, rows, pl.ds(kw, width)] = tok[:, pl.ds(TC * kw, width)]
    for c in range(1, TC):
        gathered[c][core, col, rows, :] = tok[:, pl.ds(c * kw, kw)]

    peers = [dev(x, (z + d) % Z, y, core) for d in range(1, Z)]
    xdev, ydev, cdev = dev(xf, z, y, core), dev(x, z, yf, core), dev(x, z, y, 1 - core)
    barrier = pltpu.get_barrier_semaphore()
    for peer in peers + [xdev, ydev, cdev]:
        pl.semaphore_signal(barrier, inc=1, device_id=peer, device_id_type=MESH)
    pl.semaphore_wait(barrier, Z + 2)

    def remote(src, dst, ssem, rsem, peer):
        return pltpu.make_async_remote_copy(
            src_ref=src, dst_ref=dst, send_sem=ssem, recv_sem=rsem,
            device_id=peer, device_id_type=MESH,
        )

    n1x, n1y = (1 - core) * xf + core * x, (1 - core) * y + core * yf
    n2x, n2y = (1 - core) * x + core * xf, (1 - core) * yf + core * y
    n1, n2 = dev(n1x, z, n1y, core), dev(n2x, z, n2y, core)
    n1col, n2col, diag = n1x * 2 + n1y, n2x * 2 + n2y, xf * 2 + yf

    def zsend(c, d):
        block = gathered[c].at[core, col, rows]
        return remote(block, block, zs.at[c, d - 1], zr.at[c, d - 1], peers[d - 1])

    def zrecv(c, d):
        src = pl.ds(pl.multiple_of(((z + Z - d) % Z) * 16, 16), 16)
        block = gathered[c].at[core, col, src]
        return remote(block, block, zs.at[c, d - 1], zr.at[c, d - 1], peers[d - 1])

    def hop1(c, which):
        block = gathered[c].at[core, which]
        return remote(block, block, h1s.at[c], h1r.at[c], n1)

    def hop2(c, i, which):
        block = gathered[c].at[core, which]
        return remote(block, block, h2s.at[c, i], h2r.at[c, i], n2)

    def cross(c, which):
        block = gathered[c].at[which]
        return remote(block, block, cs.at[c], cr.at[c], cdev)

    for c in range(TC):
        for d in range(1, Z):
            zsend(c, d).start()

    o = lax.broadcasted_iota(jnp.int32, (256, 256), 0)
    i = lax.broadcasted_iota(jnp.int32, (256, 256), 1)
    target = ((o & 63) >> 2) * 16 + (o & 3) * FOLD + (o >> 6)
    perm = jnp.where(i == target, 1.0, 0.0).astype(BF16)

    def compute(c):
        for cc in range(2):
            codes = gathered[c][cc].reshape(256, gathered[c].shape[3])
            moved = jnp.dot(perm, codes, preferred_element_type=F32)
            if c == 0:
                fac[pl.ds(cc * 64, 64), :] = moved[:64, kw:]
            for q in range(FOLD):
                left[q, pl.ds(cc * 64, 64), :] = moved[q * 64:(q + 1) * 64, :kw].astype(BF16)
        wcopy(c, 0).wait()
        wcopy(c, 1).wait()
        if c == 0:
            acc_g[...] = jnp.zeros_like(acc_g)
            acc_u[...] = jnp.zeros_like(acc_u)

        def step(q, carry):
            acc_g[...] += jnp.dot(left[q], gbuf[c, q], preferred_element_type=F32)
            acc_u[...] += jnp.dot(left[q], ubuf[c, q], preferred_element_type=F32)
            return carry

        lax.fori_loop(0, FOLD, step, 0)

    for s in range(TC + 3):
        if s < TC:
            for d in range(1, Z):
                zrecv(s, d).wait_recv()
            hop1(s, col).start()
        if 0 <= s - 1 < TC:
            hop1(s - 1, n1col).wait_recv()
            hop2(s - 1, 0, col).start()
            hop2(s - 1, 1, n1col).start()
        if 0 <= s - 2 < TC:
            hop2(s - 2, 0, n2col).wait_recv()
            hop2(s - 2, 1, diag).wait_recv()
            cross(s - 2, core).start()
        if 0 <= s - 3 < TC:
            cross(s - 3, 1 - core).wait_recv()
            compute(s - 3)

    factor = fac[:, 0:1]
    gate = acc_g[...] * factor * gs[:, pl.ds(off, half)]
    up = acc_u[...] * factor * us[:, pl.ds(off, half)]
    hidden = (gate / (1.0 + jnp.exp(-gate)) * up).astype(BF16)
    hid[...] = hidden.reshape(2, 2, 32, half)

    def exchange(which):
        return remote(
            hid.at[:, 1 - which, :, pl.ds(pl.multiple_of(which * (half - rest), 128), rest)],
            full.at[:, :, pl.ds(pl.multiple_of(which * half, 128), rest)],
            hs, hr, xdev,
        )

    exchange(x).start()
    full[:, :, pl.ds(off, half)] = hid[:, x]
    exchange(xf).wait_recv()

    def r1(n):
        return remote(s1s.at[n], s1r.at[n], r1s.at[n], r1r.at[n], cdev)

    def r2(n):
        return remote(s2s.at[n], s2r.at[n], r2s.at[n], r2r.at[n], ydev)

    def r3(n, d):
        return remote(
            s3s.at[n, (z + d) % Z], s3r.at[n, d - 1], r3s.at[n, d - 1], r3r.at[n, d - 1],
            peers[d - 1],
        )

    cw = ncol // FOLD
    for s in range(NC + 3):
        if s < NC:
            n = s
            dcopy(n).wait()
            product = jnp.dot(
                full[...].reshape(64, ff), dbuf[n % NB], preferred_element_type=F32
            )
            part[n] = product.reshape(2, 32, ncol)
            s1s[n] = part[n, 1 - core].astype(BF16)
            r1(n).start()
            if n + NB < NC:
                dcopy(n + NB).start()
        if 0 <= s - 1 < NC:
            n = s - 1
            r1(n).wait_recv()
            part2[n] = (part[n, core] + s1r[n].astype(F32)).reshape(2, 16, ncol)
            s2s[n] = part2[n, 1 - y].astype(BF16)
            r2(n).start()
        if 0 <= s - 2 < NC:
            n = s - 2
            r2(n).wait_recv()
            v = part2[n, y] + s2r[n].astype(F32)
            for zz in range(Z):
                block = jnp.concatenate(
                    [v[zz * 4:(zz + 1) * 4, j * cw:(j + 1) * cw] for j in range(FOLD)], axis=0
                )
                part3[n, zz] = block
                s3s[n, zz] = block.astype(BF16)
            for d in range(1, Z):
                r3(n, d).start()
        if 0 <= s - 3 < NC:
            n = s - 3
            for d in range(1, Z):
                r3(n, d).wait_recv()
            total = part3[n, z]
            for d in range(1, Z):
                total += s3r[n, d - 1].astype(F32)
            out[n] = total

    for c in range(TC):
        for d in range(1, Z):
            zsend(c, d).wait_send()
        hop1(c, col).wait_send()
        hop2(c, 0, col).wait_send()
        hop2(c, 1, n1col).wait_send()
        cross(c, core).wait_send()
    exchange(x).wait_send()
    for n in range(NC):
        r1(n).wait_send()
        r2(n).wait_send()
        for d in range(1, Z):
            r3(n, d).wait_send()


def local(
    tokens, token_scale, gate_weight, up_weight, gate_scale, up_scale, down_weight, down_scale
):
    rows, depth = tokens.shape
    ff = gate_weight.shape[1]
    half = (ff // 128 + 1) // 2 * 128
    kw = depth // FOLD // TC
    ncol = depth // NC
    lanes = 128
    codes = jnp.concatenate(
        [
            tokens.reshape(rows * FOLD, depth // FOLD),
            jnp.broadcast_to(token_scale[:, None, None], (rows, FOLD, lanes)).reshape(-1, lanes),
        ],
        axis=1,
    )
    vmem = pl.BlockSpec(memory_space=pltpu.VMEM)
    hbm = pl.BlockSpec(memory_space=pl.ANY)
    dma = pltpu.SemaphoreType.DMA
    cw = ncol // FOLD
    sums = pl.pallas_call(
        kernel,
        out_shape=jax.ShapeDtypeStruct((NC, 16, cw), F32),
        in_specs=[vmem, hbm, hbm, vmem, vmem, hbm],
        out_specs=vmem,
        scratch_shapes=[
            pltpu.VMEM((2, 4, 64, kw + lanes), BF16),
            pltpu.VMEM((2, 4, 64, kw), BF16),
            pltpu.VMEM((2, 4, 64, kw), BF16),
            pltpu.VMEM((2, 4, 64, kw), BF16),
            pltpu.VMEM((FOLD, 128, kw), BF16),
            pltpu.VMEM((128, lanes), F32),
            pltpu.VMEM((TC, FOLD, kw, half), BF16),
            pltpu.VMEM((TC, FOLD, kw, half), BF16),
            pltpu.VMEM((NB, ff, ncol), BF16),
            pltpu.VMEM((128, half), F32),
            pltpu.VMEM((128, half), F32),
            pltpu.VMEM((2, 2, 32, half), BF16),
            pltpu.VMEM((2, 32, ff), BF16),
            pltpu.VMEM((NC, 2, 32, ncol), F32),
            pltpu.VMEM((NC, 32, ncol), BF16),
            pltpu.VMEM((NC, 32, ncol), BF16),
            pltpu.VMEM((NC, 2, 16, ncol), F32),
            pltpu.VMEM((NC, 16, ncol), BF16),
            pltpu.VMEM((NC, 16, ncol), BF16),
            pltpu.VMEM((NC, Z, 16, cw), F32),
            pltpu.VMEM((NC, Z, 16, cw), BF16),
            pltpu.VMEM((NC, Z - 1, 16, cw), BF16),
            dma((2, TC)),
            dma((NC,)),
            dma((TC, Z - 1)),
            dma((TC, Z - 1)),
            dma((TC,)),
            dma((TC,)),
            dma((TC, 2)),
            dma((TC, 2)),
            dma((TC,)),
            dma((TC,)),
            dma,
            dma,
            dma((NC,)),
            dma((NC,)),
            dma((NC,)),
            dma((NC,)),
            dma((NC, Z - 1)),
            dma((NC, Z - 1)),
        ],
        compiler_params=pltpu.CompilerParams(
            collective_id=0, has_side_effects=True, vmem_limit_bytes=62 << 20
        ),
        name="ffn",
    )(
        codes,
        gate_weight.reshape(FOLD, depth // FOLD, ff),
        up_weight.reshape(FOLD, depth // FOLD, ff),
        gate_scale[None, :],
        up_scale[None, :],
        down_weight,
    )
    scale = down_scale.reshape(NC, FOLD, 1, cw)
    mixed = (sums.reshape(NC, FOLD, rows, cw) * scale).astype(BF16)
    return mixed.transpose(2, 0, 1, 3).reshape(rows, depth)


def dispatch(tokens, token_scale, gate_weight, *others):
    rows, depth = tokens.shape
    ff = gate_weight.shape[1]
    fits = (
        lax.axis_size("grp") == 2
        and lax.axis_size("inner") == 2 * Y * Z
        and rows == 4
        and depth % (FOLD * TC * 128) == 0
        and depth % (NC * FOLD * 128) == 0
        and ff % 128 == 0
        and ff > 128
    )
    form = local if fits else plain
    return form(tokens, token_scale, gate_weight, *others)


def solution(mesh):
    return jax.shard_map(
        dispatch,
        mesh=mesh,
        in_specs=(
            P(("grp", "inner"), None),
            P(("grp", "inner")),
            P(None, "inner"),
            P(None, "inner"),
            P("inner"),
            P("inner"),
            P("inner", None),
            P(),
        ),
        out_specs=P(("grp", "inner"), None),
        check_vma=False,
    )
```

time: 190 us -> 69.2 us (0.36)
  waiting for transfers between devices: 102 us -> 0 us
  Pallas kernels: 0 us -> 62.2 us
  blocking collectives: 35.1 us -> 0 us
  matrix products: 33.3 us -> 0 us
  between operations: 14.7 us -> 0.03 us
    unnamed x3 -> x0, waiting for transfers between devices: 97 us -> none
    pallas_call x0 -> x1, Pallas kernels: none -> 62.2 us  [local(): pl.pallas_call(kernel, out_shape=jax.ShapeDtypeStruct((NC, 16, cw), F32),...]
    unnamed x1 -> x0, blocking collectives: 35.1 us -> none
    dot_general x2 -> x0, matrix products: 33.3 us -> none  [the longest x1 22 us: local(): jnp.dot(hidden, down_weight, preferred_element_type=jnp.float32)]
    all_gather x1 -> x0, waiting for transfers between devices: 4.97 us -> none  [local(): pieces = lax.all_gather((tokens, token_scale), 'inner', axis=0, tiled=True)]
    unnamed x8 -> x2, local copies, waits for them, and re-layouts: 3.53 us -> 0.01 us
    broadcast_in_dim x0 -> x5, local copies, waits for them, and re-layouts: none -> 3.48 us  [the longest x1 1.3 us: local(): up_scale[None, :]]
  transfers between devices with their start and end apart: 2 -> 0, of which waited for: 2 -> 0; matrix products, arithmetic and copies ran while one was open for 1% -> 0% of each run, Pallas kernels for 0% -> 0%
where the time goes in v1:
time: 69.2 us; the launch traced here: 68.9 us
  Pallas kernels  62.2 us (90%)
  local copies, waits for them, and re-layouts  5.33 us (8%)
  other arithmetic  1.31 us (2%)
    pallas_call x1, Pallas kernels, local(): pl.pallas_call(kernel, out_shape=jax.ShapeDtypeStruct((NC, 16, cw), F32),...  62.2 us

profile of v1, /device:TPU:0, one launch (start us, length us, event | category | flops | bytes accessed | tf_op | source)
XLA Modules:
  0.0 68.9 jit_solution(15043634043512215325)
XLA Ops:
  0.0 0.9 %reshape.20 = bf16[16,2048]{1,0:T(8,128)(2,1)S(1)} reshape(bf16[4,8192]{1,0:T(4,128)(2,1)} %param.8) | data formatting | bytes 131072 | tf_op jit(solution)/shard_map/reshape | solution.py:272
  0.9 0.7 %broadcast_in_dim.16 = bf16[4,4]{1,0:T(4,128)(2,1)S(1)} broadcast(bf16[4]{0:T(256)(128)(2,1)} %param.9), dimensions={0} | broadcast | bytes 40 | tf_op jit(solution)/shard_map/broadcast_in_dim | solution.py:273
  1.6 0.1 broadcast_in_dim.17
  1.7 0.1 broadcast_in_dim.18
  1.8 0.6 pad_maximum_fusion.tok
  2.4 1.3 %broadcast_in_dim.19.gs = f32[1,1664]{1,0:T(1,128)} reshape(f32[1664]{0:T(1024)} %param.12) | data formatting | bytes 13312 | tf_op jit(solution)/shard_map/broadcast_in_dim | solution.py:336
  3.7 1.3 %broadcast_in_dim.20.us = f32[1,1664]{1,0:T(1,128)} reshape(f32[1664]{0:T(1024)} %param.13) | data formatting | bytes 13312 | tf_op jit(solution)/shard_map/broadcast_in_dim | solution.py:337
  5.0 0.0 copy-start
  5.0 62.2 %ffn.1 = f32[8,16,256]{2,1,0:T(8,128)} custom-call(bf16[16,2176]{1,0:T(8,128)(2,1)} %pad_maximum_fusion.tok, bf16[4,2048,1664]{2,1,0:T(8,128)(2,1)} %bitcast.5, bf16[4,2048,1664]{2,1,0:T(8,128)(2,1)} %bitcast.6, f32[1,1664]{1,0:T(1,128)} %broadcast_in_dim.19.gs, f32[1,1664]{1,0:T(1,128)} %broadcast_in_dim.20.us, bf16[1664,8192]{1,0:T(8,128)(2,1)} %dw.1), custom_call_target="tpu_custom_call" | custom-call | tf_op jit(solution)/shard_map/ffn/pallas_call | solution.py:281
  67.2 0.9 %reshape.23 = f32[8,4,4,256]{3,2,1,0:T(4,128)S(1)} reshape(f32[8,16,256]{2,1,0:T(8,128)} %ffn.1) | data formatting | bytes 262144 | tf_op jit(solution)/shard_map/reshape | solution.py:341
  68.2 0.0 copy-done
  68.2 0.7 multiply_convert_fusion
  (1 shorter events, 0.0 us)
Async XLA Ops:
  5.0 63.2 %copy-start = (f32[8192]{0:T(1024)S(1)}, f32[8192]{0:T(1024)}, u32[]{:S(2)}) copy-start(f32[8192]{0:T(1024)} %param.15) | copy-start | bytes 98308

commit v2 on v1

--- a/solution.py
+++ b/solution.py
@@ -11,8 +11,9 @@
 FOLD = 4
 TC = 4
 NC = 8
-NB = 5
+NB = 6
 Z, Y = 4, 2
+LAG = (2, 5, 8)
 
 
 def plain(
@@ -45,7 +46,7 @@
     tok, gw, uw, gs, us, dw, out,
     g0, g1, g2, g3, left, fac, gbuf, ubuf, dbuf, acc_g, acc_u, hid, full,
     part, s1s, s1r, part2, s2s, s2r, part3, s3s, s3r,
-    wsem, dsem, zs, zr, h1s, h1r, h2s, h2r, cs, cr, hs, hr, r1s, r1r, r2s, r2r, r3s, r3r,
+    wsem, dsem, zs, zr, h1s, h1r, cs, cr, hs, hr, r1s, r1r, r2s, r2r, r3s, r3r,
 ):
     x = lax.axis_index("grp")
     inner = lax.axis_index("inner")
@@ -90,10 +91,11 @@
 
     peers = [dev(x, (z + d) % Z, y, core) for d in range(1, Z)]
     xdev, ydev, cdev = dev(xf, z, y, core), dev(x, z, yf, core), dev(x, z, y, 1 - core)
+    ddev = dev(xf, z, yf, core)
     barrier = pltpu.get_barrier_semaphore()
-    for peer in peers + [xdev, ydev, cdev]:
+    for peer in peers + [xdev, ydev, ddev, cdev]:
         pl.semaphore_signal(barrier, inc=1, device_id=peer, device_id_type=MESH)
-    pl.semaphore_wait(barrier, Z + 2)
+    pl.semaphore_wait(barrier, Z + 3)
 
     def remote(src, dst, ssem, rsem, peer):
         return pltpu.make_async_remote_copy(
@@ -101,10 +103,7 @@
             device_id=peer, device_id_type=MESH,
         )
 
-    n1x, n1y = (1 - core) * xf + core * x, (1 - core) * y + core * yf
-    n2x, n2y = (1 - core) * x + core * xf, (1 - core) * yf + core * y
-    n1, n2 = dev(n1x, z, n1y, core), dev(n2x, z, n2y, core)
-    n1col, n2col, diag = n1x * 2 + n1y, n2x * 2 + n2y, xf * 2 + yf
+    plane = [(xdev, xf * 2 + y), (ydev, x * 2 + yf), (ddev, xf * 2 + yf)]
 
     def zsend(c, d):
         block = gathered[c].at[core, col, rows]
@@ -115,13 +114,9 @@
         block = gathered[c].at[core, col, src]
         return remote(block, block, zs.at[c, d - 1], zr.at[c, d - 1], peers[d - 1])
 
-    def hop1(c, which):
+    def spread(c, k, which):
         block = gathered[c].at[core, which]
-        return remote(block, block, h1s.at[c], h1r.at[c], n1)
-
-    def hop2(c, i, which):
-        block = gathered[c].at[core, which]
-        return remote(block, block, h2s.at[c, i], h2r.at[c, i], n2)
+        return remote(block, block, h1s.at[c, k], h1r.at[c, k], plane[k][0])
 
     def cross(c, which):
         block = gathered[c].at[which]
@@ -157,26 +152,23 @@
 
         lax.fori_loop(0, FOLD, step, 0)
 
-    for s in range(TC + 3):
+    for c in range(TC):
+        for d in range(1, Z):
+            zrecv(c, d).wait_recv()
+        for k in range(3):
+            spread(c, k, col).start()
+    for s in range(TC + 1):
         if s < TC:
-            for d in range(1, Z):
-                zrecv(s, d).wait_recv()
-            hop1(s, col).start()
-        if 0 <= s - 1 < TC:
-            hop1(s - 1, n1col).wait_recv()
-            hop2(s - 1, 0, col).start()
-            hop2(s - 1, 1, n1col).start()
-        if 0 <= s - 2 < TC:
-            hop2(s - 2, 0, n2col).wait_recv()
-            hop2(s - 2, 1, diag).wait_recv()
-            cross(s - 2, core).start()
-        if 0 <= s - 3 < TC:
-            cross(s - 3, 1 - core).wait_recv()
-            compute(s - 3)
+            for k in range(3):
+                spread(s, k, plane[k][1]).wait_recv()
+            cross(s, core).start()
+        if s >= 1:
+            cross(s - 1, 1 - core).wait_recv()
+            compute(s - 1)
 
     factor = fac[:, 0:1]
-    gate = acc_g[...] * factor * gs[:, pl.ds(off, half)]
-    up = acc_u[...] * factor * us[:, pl.ds(off, half)]
+    gate = acc_g[...] * factor * jnp.where(x == 0, gs[0:half], gs[rest:ff])[None, :]
+    up = acc_u[...] * factor * jnp.where(x == 0, us[0:half], us[rest:ff])[None, :]
     hidden = (gate / (1.0 + jnp.exp(-gate)) * up).astype(BF16)
     hid[...] = hidden.reshape(2, 2, 32, half)
 
@@ -189,7 +181,13 @@
 
     exchange(x).start()
     full[:, :, pl.ds(off, half)] = hid[:, x]
+    own = hid[:, x].reshape(64, half)
+    for n in range(NB):
+        dcopy(n).wait()
+        product = jnp.dot(own, dbuf[n, pl.ds(off, half), :], preferred_element_type=F32)
+        part[n] = product.reshape(2, 32, ncol)
     exchange(xf).wait_recv()
+    far = pl.ds(pl.multiple_of((1 - x) * half, 128), rest)
 
     def r1(n):
         return remote(s1s.at[n], s1r.at[n], r1s.at[n], r1r.at[n], cdev)
@@ -204,26 +202,33 @@
         )
 
     cw = ncol // FOLD
-    for s in range(NC + 3):
+    for s in range(NC + LAG[2]):
         if s < NC:
             n = s
-            dcopy(n).wait()
-            product = jnp.dot(
-                full[...].reshape(64, ff), dbuf[n % NB], preferred_element_type=F32
-            )
-            part[n] = product.reshape(2, 32, ncol)
+            if n < NB:
+                product = jnp.dot(
+                    full[:, :, far].reshape(64, rest), dbuf[n, far, :],
+                    preferred_element_type=F32,
+                )
+                part[n] += product.reshape(2, 32, ncol)
+            else:
+                dcopy(n).wait()
+                product = jnp.dot(
+                    full[...].reshape(64, ff), dbuf[n % NB], preferred_element_type=F32
+                )
+                part[n] = product.reshape(2, 32, ncol)
             s1s[n] = part[n, 1 - core].astype(BF16)
             r1(n).start()
             if n + NB < NC:
                 dcopy(n + NB).start()
-        if 0 <= s - 1 < NC:
-            n = s - 1
+        if 0 <= s - LAG[0] < NC:
+            n = s - LAG[0]
             r1(n).wait_recv()
             part2[n] = (part[n, core] + s1r[n].astype(F32)).reshape(2, 16, ncol)
             s2s[n] = part2[n, 1 - y].astype(BF16)
             r2(n).start()
-        if 0 <= s - 2 < NC:
-            n = s - 2
+        if 0 <= s - LAG[1] < NC:
+            n = s - LAG[1]
             r2(n).wait_recv()
             v = part2[n, y] + s2r[n].astype(F32)
             for zz in range(Z):
@@ -234,8 +239,8 @@
                 s3s[n, zz] = block.astype(BF16)
             for d in range(1, Z):
                 r3(n, d).start()
-        if 0 <= s - 3 < NC:
-            n = s - 3
+        if 0 <= s - LAG[2] < NC:
+            n = s - LAG[2]
             for d in range(1, Z):
                 r3(n, d).wait_recv()
             total = part3[n, z]
@@ -246,9 +251,8 @@
     for c in range(TC):
         for d in range(1, Z):
             zsend(c, d).wait_send()
-        hop1(c, col).wait_send()
-        hop2(c, 0, col).wait_send()
-        hop2(c, 1, n1col).wait_send()
+        for k in range(3):
+            spread(c, k, col).wait_send()
         cross(c, core).wait_send()
     exchange(x).wait_send()
     for n in range(NC):
@@ -310,10 +314,8 @@
             dma((NC,)),
             dma((TC, Z - 1)),
             dma((TC, Z - 1)),
-            dma((TC,)),
-            dma((TC,)),
-            dma((TC, 2)),
-            dma((TC, 2)),
+            dma((TC, 3)),
+            dma((TC, 3)),
             dma((TC,)),
             dma((TC,)),
             dma,
@@ -333,8 +335,8 @@
         codes,
         gate_weight.reshape(FOLD, depth // FOLD, ff),
         up_weight.reshape(FOLD, depth // FOLD, ff),
-        gate_scale[None, :],
-        up_scale[None, :],
+        gate_scale,
+        up_scale,
         down_weight,
     )
     scale = down_scale.reshape(NC, FOLD, 1, cw)

time: 69.2 us -> 53.7 us (0.78)
  Pallas kernels: 62.2 us -> 49.4 us
  local copies, waits for them, and re-layouts: 5.33 us -> 2.74 us
    pallas_call x1, Pallas kernels: 62.2 us -> 49.4 us  [local(): pl.pallas_call(kernel, out_shape=jax.ShapeDtypeStruct((NC, 16, cw), F32),...]
    broadcast_in_dim x2 -> x0, local copies, waits for them, and re-layouts: 2.59 us -> none  [the longest x1 1.3 us: local(): up_scale[None, :]]
where the time goes in v2:
time: 53.7 us; the launch traced here: 53.5 us
  Pallas kernels  49.4 us (92%)
  local copies, waits for them, and re-layouts  2.74 us (5%)
  other arithmetic  1.31 us (2%)
    pallas_call x1, Pallas kernels, local(): pl.pallas_call(kernel, out_shape=jax.ShapeDtypeStruct((NC, 16, cw), F32),...  49.4 us

profile of v2, /device:TPU:0, one launch (start us, length us, event | category | flops | bytes accessed | tf_op | source)
XLA Modules:
  0.0 53.5 jit_solution(4362966148329406412)
XLA Ops:
  0.0 0.9 %reshape.20 = bf16[16,2048]{1,0:T(8,128)(2,1)S(1)} reshape(bf16[4,8192]{1,0:T(4,128)(2,1)} %param.8) | data formatting | bytes 131072 | tf_op jit(solution)/shard_map/reshape | solution.py:276
  0.9 0.7 %broadcast_in_dim.10 = bf16[4,4]{1,0:T(4,128)(2,1)S(1)} broadcast(bf16[4]{0:T(256)(128)(2,1)} %param.9), dimensions={0} | broadcast | bytes 40 | tf_op jit(solution)/shard_map/broadcast_in_dim | solution.py:277
  1.6 0.1 broadcast_in_dim.11
  1.7 0.1 broadcast_in_dim.12
  1.8 0.6 %pad_maximum_fusion.tok = bf16[16,2176]{1,0:T(8,128)(2,1)} fusion(bf16[16,128]{1,0:T(8,128)(2,1)S(1)} %broadcast_in_dim.12, bf16[16,2048]{1,0:T(8,128)(2,1)S(1)} %reshape.20), kind=kLoop, calls=%fused_computation.1 | loop fusion | flops 139264 | bytes 139264 | tf_op jit(solution)/shard_map/concatenate | solution.py:274
  2.4 0.0 copy-start
  2.4 49.4 %ffn.1 = f32[8,16,256]{2,1,0:T(8,128)} custom-call(bf16[16,2176]{1,0:T(8,128)(2,1)} %pad_maximum_fusion.tok, bf16[4,2048,1664]{2,1,0:T(8,128)(2,1)} %bitcast.5, bf16[4,2048,1664]{2,1,0:T(8,128)(2,1)} %bitcast.6, f32[1664]{0:T(1024)} %gs.1, f32[1664]{0:T(1024)} %us.1, bf16[1664,8192]{1,0:T(8,128)(2,1)} %dw.1), custom_call_target="tpu_custom_call" | custom-call | tf_op jit(solution)/shard_map/ffn/pallas_call | solution.py:285
  51.8 0.9 %reshape.23 = f32[8,4,4,256]{3,2,1,0:T(4,128)S(1)} reshape(f32[8,16,256]{2,1,0:T(8,128)} %ffn.1) | data formatting | bytes 262144 | tf_op jit(solution)/shard_map/reshape | solution.py:343
  52.8 0.0 copy-done
  52.8 0.7 %multiply_convert_fusion = bf16[8,4,4,256]{3,2,1,0:T(4,128)(2,1)} fusion(f32[8,4,4,256]{3,2,1,0:T(4,128)S(1)} %reshape.23, f32[8,4,256]{2,1,0:T(4,128)S(1)} %mul.10), kind=kLoop, calls=%fused_computation | loop fusion | flops 65536 | bytes 229376 | tf_op jit(solution)/shard_map/convert_element_type | solution.py:343
  (1 shorter events, 0.0 us)
Async XLA Ops:
  2.4 50.4 %copy-start = (f32[8192]{0:T(1024)S(1)}, f32[8192]{0:T(1024)}, u32[]{:S(2)}) copy-start(f32[8192]{0:T(1024)} %param.15) | copy-start | bytes 98308
